TPU v7x, 128 devices: a whole 4x4x4 slice. The times are simulated.
128 devices in a mesh: row: 16 (over y, x), col: 2 (over core), depth: 4 (over z).
Axes of the slice: x: 4, y: 4, z: 4, core: 2. Of those that a mesh axis runs over, the one named last changes fastest.
Arguments:
- amplitudes: float32 [3584, 14336], P('row', ('col', 'depth')), may hold values from -6 to 6
- intermediate: float32 [14336, 14336], P(('col', 'depth'), 'row'), may hold values from -0.046875 to 0.046875
Outputs:
- sigma_cycle: float32 [3584, 14336], P(('col', 'depth'), 'row')
All inputs are finite; a program needn't handle non-finite values.
Results may differ from a plain program's by a relative error of at most 0.00011.
Values sent between devices are 32-bit elements; how exact they have to be, the bound alone decides.
A program may use at most 128 MiB of HBM per device.

v0:
```python
import jax
import jax.numpy as jnp
from jax import lax
from jax.sharding import PartitionSpec as P


def per_device(amplitudes, intermediate):
    gathered = lax.all_gather(amplitudes, "row", axis=0, tiled=True)
    partial_sigma = jnp.dot(
        gathered, intermediate, preferred_element_type=jnp.float32, precision=lax.Precision.HIGHEST
    )
    layer_sum = lax.psum_scatter(partial_sigma, "col", scatter_dimension=0, tiled=True)
    sigma_cycle = lax.psum_scatter(layer_sum, "depth", scatter_dimension=0, tiled=True)
    return sigma_cycle


def solution(mesh):
    return jax.shard_map(
        per_device,
        mesh=mesh,
        in_specs=(P("row", ("col", "depth")), P(("col", "depth"), "row")),
        out_specs=P(("col", "depth"), "row"),
        check_vma=False,
    )
```

profile of v0, /device:TPU:1, one launch (start us, length us, event | category | flops | bytes accessed | tf_op | source)
XLA Modules:
  0.0 359.0 jit_solution(496431679964194209)
XLA Ops:
  6.5 0.0 all-gather.2.cloned.1.call-start
  6.5 0.7 all-gather.2.cloned.1.call-update
  7.3 0.0 reduce-scatter.3.cloned.1.call-start
  7.3 162.2 %all-gather.2.cloned.1.call-done = f32[3584,1792]{1,0:T(8,128)} async-done(((f32[224,1792]{1,0:T(8,128)}), f32[3584,1792]{1,0:T(8,128)}) %all-gather.2.cloned.1.call-update) | async-done | bytes 25690128 | tf_op jit(solution)/shard_map/all_gather | solution.py:8
  169.5 89.5 %fusion = f32[3584,896]{1,0:T(8,128)} fusion(f32[3584,1792]{1,0:T(8,128)} %all-gather.2.cloned.1.call-done, f32[1792,896]{1,0:T(8,128)} %param.3), kind=kOutput, calls=%fused_computation | convolution fusion | flops 69055021056 | bytes 44957696 | tf_op jit(solution)/shard_map/dot_general | solution.py:9
  259.0 0.0 reduce-scatter.3.cloned.1.call-update
  259.0 0.0 reduce-scatter.5.cloned.1.call-start
  259.1 24.7 %reduce-scatter.3.cloned.1.call-done = f32[1792,896]{1,0:T(8,128)} async-done(((f32[3584,896]{1,0:T(8,128)}), f32[1792,896]{1,0:T(8,128)}) %reduce-scatter.3.cloned.1.call-update) | async-done | bytes 6422544 | tf_op jit(solution)/shard_map/reduce_scatter | solution.py:12
  283.7 0.0 reduce-scatter.5.cloned.1.call-update
  283.8 68.7 %reduce-scatter.5.cloned.1.call-done = f32[448,896]{1,0:T(8,128)} async-done(((f32[1792,896]{1,0:T(8,128)}), f32[448,896]{1,0:T(8,128)}) %reduce-scatter.5.cloned.1.call-update) | async-done | bytes 1605648 | tf_op jit(solution)/shard_map/reduce_scatter | solution.py:13
Async XLA Ops:
  6.5 162.9 %all-gather.2.cloned.1.call-start = ((), (), s32[]{:S(2)}) async-start(), calls=%async_computation.2 | async-start | bytes 27295744 | tf_op jit(solution)/shard_map/all_gather | solution.py:8
  7.3 276.5 %reduce-scatter.3.cloned.1.call-start = ((), (), s32[]{:S(2)}) async-start(), calls=%async_computation.3 | async-start | bytes 19267584 | tf_op jit(solution)/shard_map/reduce_scatter | solution.py:12
  259.0 93.5 %reduce-scatter.5.cloned.1.call-start = ((), (), s32[]{:S(2)}) async-start(), calls=%async_computation.4 | async-start | bytes 8028160 | tf_op jit(solution)/shard_map/reduce_scatter | solution.py:13
Sparse Core Ops, SparseCore 0:
  9.5 159.9 all-gather.1
  259.1 24.5 reduce-scatter.2
  286.2 66.2 reduce-scatter.4
where the time goes:
time: 359 us
  waiting for transfers between devices  256 us (71%)
  matrix products  89.5 us (25%)
  between operations  13.1 us (4%)
    all_gather x1, waiting for transfers between devices, per_device(): gathered = lax.all_gather(amplitudes, 'row', axis=0, tiled=True)  162 us
    dot_general x1, matrix products, per_device(): jnp.dot(gathered, intermediate, preferred_element_type=jnp.float32, preci...  89.5 us
    reduce_scatter x1, waiting for transfers between devices, per_device(): lax.psum_scatter(layer_sum, 'depth', scatter_dimension=0, tiled=True)  68.7 us
    reduce_scatter x1, waiting for transfers between devices, per_device(): lax.psum_scatter(partial_sigma, 'col', scatter_dimension=0, tiled=True)  24.7 us
  transfers between devices with their start and end apart: 3, of which 3 were waited for; matrix products, arithmetic and copies ran while one was open for 0% of the time, Pallas kernels for 0%

commit v1 on v0

v1 whole, which is shorter than its diff:
```python
import functools

import jax
import jax.numpy as jnp
from jax import lax
from jax.experimental import pallas as pl
from jax.experimental.pallas import tpu as pltpu
from jax.sharding import PartitionSpec as P

MESH = pl.DeviceIdType.MESH

D1 = (0, 1, 3, 0, 2, 1, 3, 2, 0, 1, 3, 2, 2, 0, 1, 3)
D2 = (0, 0, 0, 1, 0, 1, 1, 1, 3, 3, 3, 3, 2, 2, 2, 2)
PARENT = (0, 0, 0, 0, 1, 1, 2, 4, 0, 1, 2, 4, 7, 3, 5, 6)
STEP1 = (0, 1, -1, 0, 1, 0, 0, 0, 0, 0, 0, 0, 0, 0, 0, 0)
STEP2 = (0, 0, 0, 1, 0, 1, 1, 1, -1, -1, -1, -1, 1, 1, 1, 1)
WAVES = 16
AHEAD = 3
PIECES = 4


def look_up(table, w):
    if isinstance(w, int):
        return table[w]
    value = jnp.int32(table[0])
    for k in range(1, len(table)):
        if table[k] != table[0]:
            value = jnp.where(w == k, jnp.int32(table[k]), value)
    return value


def kernel(a_ref, b_ref, out_ref, g, p, s, r, f, a_hi, a_lo, b_hi, b_lo,
           in_sem, g_send, g_recv, s_send, s_recv, z_send, r_recv, f_recv, out_sem):
    row, core, z = lax.axis_index("row"), lax.axis_index("col"), lax.axis_index("depth")
    y, x = row // 4, row % 4
    piece_rows = a_ref.shape[1]
    depth, columns = b_ref.shape
    block_rows = PIECES * piece_rows

    own = [pltpu.make_async_copy(a_ref.at[q], g.at[0, q], in_sem.at[q]) for q in range(PIECES)]
    for copy in own:
        copy.start()
    stage_waves = depth // block_rows
    b_copies = [
        pltpu.make_async_copy(
            b_ref.at[pl.ds((4 * k + q) * piece_rows, piece_rows)], p.at[WAVES - stage_waves + k, q], in_sem.at[PIECES + 4 * k + q]
        )
        for k in range(stage_waves)
        for q in range(PIECES)
    ]
    for copy in b_copies:
        copy.start()

    def at_row(yy, xx):
        return {"row": ((yy + 8) % 4) * 4 + (xx + 8) % 4}

    barrier = pltpu.get_barrier_semaphore()
    neighbours = [at_row(y, x + 1), at_row(y, x - 1), at_row(y + 1, x), at_row(y - 1, x),
                  {"col": 1 - core}, {"depth": (z + 1) % 4}, {"depth": (z + 3) % 4}]
    for device in neighbours:
        pl.semaphore_signal(barrier, inc=1, device_id=device, device_id_type=MESH)
    pl.semaphore_wait(barrier, len(neighbours))

    def sign(q):
        return 1 - 2 * (q % 2)

    def gather_copy(w, q):
        s1, s2 = sign(q) * look_up(STEP1, w), sign(q) * look_up(STEP2, w)
        sx, sy = (s1, s2) if q < 2 else (s2, s1)
        return pltpu.make_async_remote_copy(
            src_ref=g.at[look_up(PARENT, w), q], dst_ref=g.at[w, q], send_sem=g_send.at[w, q], recv_sem=g_recv.at[w, q],
            device_id=at_row(y + sy, x + sx), device_id_type=MESH,
        )

    def origin(w, q):
        d1, d2 = look_up(D1, w), look_up(D2, w)
        dx, dy = (d1, d2) if q < 2 else (d2, d1)
        xs, ys = (x + 8 - sign(q) * dx) % 4, (y + 8 - sign(q) * dy) % 4
        pair = d1 * 2 + d2 % 2 if q < 2 else (d1 % 2) * 4 + d2
        return ys // 2, 2 * (ys % 2) + xs // 2, xs % 2, pair

    def core_copy(w, q, pair):
        return pltpu.make_async_remote_copy(
            src_ref=p.at[w, q], dst_ref=s.at[pair, q], send_sem=s_send.at[pair, q], recv_sem=s_recv.at[pair, q],
            device_id={"col": 1 - core}, device_id_type=MESH,
        )

    def relay_copy(w, q, half):
        return pltpu.make_async_remote_copy(
            src_ref=p.at[w, q], dst_ref=r.at[half, q], send_sem=z_send.at[1, half, q], recv_sem=r_recv.at[half, q],
            device_id={"depth": (z + 4 + sign(q)) % 4}, device_id_type=MESH,
        )

    def final_copy(w, q, half, which):
        step = -sign(q) if which == 0 else sign(q)
        return pltpu.make_async_remote_copy(
            src_ref=p.at[w, q], dst_ref=f.at[which, half, q], send_sem=z_send.at[2 * which, half, q],
            recv_sem=f_recv.at[which, half, q], device_id={"depth": (z + 4 + step) % 4}, device_id_type=MESH,
        )

    def out_copy(w, q, half):
        return pltpu.make_async_copy(p.at[w, q], out_ref.at[half, q], out_sem.at[half, q])

    def relation(dest_z, q):
        return ((dest_z - z + 4) * sign(q) + 16) % 4

    def send_wave(w):
        for q in range(PIECES):
            gather_copy(w, q).start()

    for copy in own:
        copy.wait()
    for w in range(1, AHEAD + 1):
        send_wave(w)

    for copy in b_copies:
        copy.wait()

    @pl.loop(0, stage_waves)
    def _(k):
        b = p[WAVES - stage_waves + k].reshape(block_rows, columns)
        hi = b.astype(jnp.bfloat16)
        b_hi[pl.ds(pl.multiple_of(k * block_rows, 32), block_rows)] = hi
        b_lo[pl.ds(pl.multiple_of(k * block_rows, 32), block_rows)] = (b - hi.astype(jnp.float32)).astype(jnp.bfloat16)

    def multiply(w):
        for k0 in range(0, depth, 256):
            a = g[w, :, :, k0:k0 + 256].reshape(block_rows, 256)
            hi = a.astype(jnp.bfloat16)
            a_hi[:, k0:k0 + 256] = hi
            a_lo[:, k0:k0 + 256] = (a - hi.astype(jnp.float32)).astype(jnp.bfloat16)
        dot = functools.partial(jnp.dot, preferred_element_type=jnp.float32)
        for n0 in range(0, columns, 256):
            n1 = min(n0 + 256, columns)
            total = dot(a_hi[...], b_hi[:, n0:n1]) + (dot(a_hi[...], b_lo[:, n0:n1]) + dot(a_lo[...], b_hi[:, n0:n1]))
            p[w, :, :, n0:n1] = total.reshape(PIECES, piece_rows, n1 - n0)

    def stage_core(w):
        for q in range(PIECES):
            dest_core, dest_z, half, pair = origin(w, q)
            kind = relation(dest_z, q)

            @pl.when(dest_core == core)
            def _():
                core_copy(w, q, pair).wait_recv()
                p[w, q] = p[w, q] + s[pair, q]

                @pl.when(kind == 2)
                def _():
                    relay_copy(w, q, half).start()

                @pl.when(kind == 3)
                def _():
                    final_copy(w, q, half, 0).start()

    def stage_relay(w):
        for q in range(PIECES):
            dest_core, dest_z, half, _ = origin(w, q)

            @pl.when((dest_core == core) & (relation(dest_z, q) == 1))
            def _():
                relay_copy(w, q, half).wait_recv()
                p[w, q] = p[w, q] + r[half, q]
                final_copy(w, q, half, 1).start()

    def stage_final(w):
        for q in range(PIECES):
            dest_core, dest_z, half, _ = origin(w, q)

            @pl.when((dest_core == core) & (relation(dest_z, q) == 0))
            def _():
                final_copy(w, q, half, 0).wait_recv()
                final_copy(w, q, half, 1).wait_recv()
                p[w, q] = p[w, q] + (f[0, half, q] + f[1, half, q])
                out_copy(w, q, half).start()

    @pl.loop(0, WAVES + 3)
    def _(w):
        @pl.when((w >= 1) & (w <= WAVES))
        def _():
            stage_core(w - 1)

        @pl.when((w >= 2) & (w <= WAVES + 1))
        def _():
            stage_relay(w - 2)

        @pl.when(w >= 3)
        def _():
            stage_final(w - 3)

        @pl.when(w < WAVES)
        def _():
            @pl.when(w >= 1)
            def _():
                for q in range(PIECES):
                    gather_copy(w, q).wait_recv()

                @pl.when(w + AHEAD < WAVES)
                def _():
                    send_wave(w + AHEAD)

            multiply(w)
            for q in range(PIECES):
                dest_core, _, _, pair = origin(w, q)

                @pl.when(dest_core != core)
                def _():
                    core_copy(w, q, pair).start()

    @pl.loop(1, WAVES)
    def _(w):
        for q in range(PIECES):
            gather_copy(w, q).wait_send()

    @pl.loop(0, 8)
    def _(pair):
        for q in range(PIECES):
            core_copy(0, q, pair).wait_send()

    for half in range(2):
        for q in range(PIECES):
            relay_copy(0, q, half).wait_send()
            final_copy(0, q, half, 0).wait_send()
            final_copy(0, q, half, 1).wait_send()
            out_copy(0, q, half).wait()


def per_device(amplitudes, intermediate):
    block_rows, depth = amplitudes.shape
    columns = intermediate.shape[1]
    rows = block_rows // PIECES
    f32, bf16 = jnp.float32, jnp.bfloat16
    dma = pltpu.SemaphoreType.DMA
    result = pl.pallas_call(
        kernel,
        out_shape=jax.ShapeDtypeStruct((2, PIECES, rows, columns), f32),
        in_specs=[pl.BlockSpec(memory_space=pl.ANY)] * 2,
        out_specs=pl.BlockSpec(memory_space=pl.ANY),
        scratch_shapes=[
            pltpu.VMEM((WAVES, PIECES, rows, depth), f32),
            pltpu.VMEM((WAVES, PIECES, rows, columns), f32),
            pltpu.VMEM((WAVES // 2, PIECES, rows, columns), f32),
            pltpu.VMEM((2, PIECES, rows, columns), f32),
            pltpu.VMEM((2, 2, PIECES, rows, columns), f32),
            pltpu.VMEM((block_rows, depth), bf16),
            pltpu.VMEM((block_rows, depth), bf16),
            pltpu.VMEM((depth, columns), bf16),
            pltpu.VMEM((depth, columns), bf16),
            dma((PIECES + 32,)),
            dma((WAVES, PIECES)),
            dma((WAVES, PIECES)),
            dma((WAVES // 2, PIECES)),
            dma((WAVES // 2, PIECES)),
            dma((3, 2, PIECES)),
            dma((2, PIECES)),
            dma((2, 2, PIECES)),
            dma((2, PIECES)),
        ],
        compiler_params=pltpu.CompilerParams(
            collective_id=0, has_side_effects=True, vmem_limit_bytes=60 * 2**20
        ),
        cost_estimate=pl.CostEstimate(flops=34_500_000_000, bytes_accessed=10_000_000, transcendentals=0),
    )(amplitudes.reshape(PIECES, rows, depth), intermediate)
    return result.reshape(2 * block_rows, columns)


def solution(mesh):
    return jax.shard_map(
        per_device,
        mesh=mesh,
        in_specs=(P("row", ("col", "depth")), P(("col", "depth"), "row")),
        out_specs=P(("col", "depth"), "row"),
        check_vma=False,
    )
```

time: 359 us -> 157 us (0.44)
  waiting for transfers between devices: 256 us -> 0 us
  Pallas kernels: 0 us -> 154 us
  matrix products: 89.5 us -> 0 us
  between operations: 13.1 us -> 0.01 us
    all_gather x1 -> x0, waiting for transfers between devices: 162 us -> none  [per_device(): gathered = lax.all_gather(amplitudes, 'row', axis=0, tiled=True)]
    pallas_call x0 -> x1, Pallas kernels: none -> 154 us  [per_device(): pl.pallas_call(kernel, out_shape=jax.ShapeDtypeStruct((2, PIECES, rows, c...]
    reduce_scatter x2 -> x0, waiting for transfers between devices: 93.4 us -> none  [the longest x1 68.7 us: per_device(): lax.psum_scatter(layer_sum, 'depth', scatter_dimension=0, tiled=True)]
    dot_general x1 -> x0, matrix products: 89.5 us -> none  [per_device(): jnp.dot(gathered, intermediate, preferred_element_type=jnp.float32, preci...]
  transfers between devices with their start and end apart: 3 -> 0, of which waited for: 3 -> 0; matrix products, arithmetic and copies ran while one was open for 0% -> 0% of each run, Pallas kernels for 0% -> 0%
where the time goes in v1:
time: 157 us
  Pallas kernels  154 us (98%)
  local copies, waits for them, and re-layouts  2.68 us (2%)
    pallas_call x1, Pallas kernels, per_device(): pl.pallas_call(kernel, out_shape=jax.ShapeDtypeStruct((2, PIECES, rows, c...  154 us

profile of v1, /device:TPU:1, one launch (start us, length us, event | category | flops | bytes accessed | tf_op | source)
XLA Modules:
  0.0 156.8 jit_solution(10189396526116881737)
XLA Ops:
  0.0 154.1 %shard_map.28 = f32[2,4,56,896]{3,2,1,0:T(8,128)} custom-call(f32[4,56,1792]{2,1,0:T(8,128)} %bitcast.3, f32[1792,896]{1,0:T(8,128)} %b_ref.1), custom_call_target="tpu_custom_call" | custom-call | flops 34500001792 | bytes 10000000 | tf_op jit(solution)/shard_map/pallas_call | solution.py:234
  154.1 2.7 %copy.4 = f32[448,896]{1,0:T(8,128)} copy(f32[448,896]{1,0:T(8,128)} %bitcast.2) | data formatting | bytes 3211264

commit v2 on v1

--- a/solution.py
+++ b/solution.py
@@ -9,28 +9,61 @@
 
 MESH = pl.DeviceIdType.MESH
 
-D1 = (0, 1, 3, 0, 2, 1, 3, 2, 0, 1, 3, 2, 2, 0, 1, 3)
-D2 = (0, 0, 0, 1, 0, 1, 1, 1, 3, 3, 3, 3, 2, 2, 2, 2)
-PARENT = (0, 0, 0, 0, 1, 1, 2, 4, 0, 1, 2, 4, 7, 3, 5, 6)
-STEP1 = (0, 1, -1, 0, 1, 0, 0, 0, 0, 0, 0, 0, 0, 0, 0, 0)
-STEP2 = (0, 0, 0, 1, 0, 1, 1, 1, -1, -1, -1, -1, 1, 1, 1, 1)
+D1 = (
+    (0, 1, 3, 0, 2, 1, 3, 2, 0, 1, 3, 2, 2, 0, 1, 3),
+    (0, 1, 3, 0, 2, 1, 3, 2, 0, 1, 3, 2, 2, 0, 1, 3),
+    (0, 1, 3, 0, 2, 1, 3, 2, 0, 1, 3, 2, 2, 0, 1, 3),
+    (0, 1, 3, 0, 2, 1, 3, 2, 0, 1, 3, 2, 2, 0, 1, 3),
+)
+D2 = (
+    (0, 0, 0, 1, 0, 1, 1, 1, 3, 3, 3, 3, 2, 2, 2, 2),
+    (0, 0, 0, 1, 0, 1, 1, 1, 3, 3, 3, 3, 2, 2, 2, 2),
+    (0, 0, 0, 1, 0, 1, 1, 1, 3, 3, 3, 3, 2, 2, 2, 2),
+    (0, 0, 0, 1, 0, 1, 1, 1, 3, 3, 3, 3, 2, 2, 2, 2),
+)
+PARENT = (
+    (0, 0, 0, 0, 1, 1, 2, 4, 0, 1, 2, 4, 7, 3, 5, 6),
+    (0, 0, 0, 0, 1, 1, 2, 4, 0, 1, 2, 4, 7, 3, 5, 6),
+    (0, 0, 0, 0, 1, 1, 2, 4, 0, 1, 2, 4, 7, 3, 5, 6),
+    (0, 0, 0, 0, 1, 1, 2, 4, 0, 1, 2, 4, 7, 3, 5, 6),
+)
+STEP1 = (
+    (0, 1, -1, 0, 1, 0, 0, 0, 0, 0, 0, 0, 0, 0, 0, 0),
+    (0, 1, -1, 0, 1, 0, 0, 0, 0, 0, 0, 0, 0, 0, 0, 0),
+    (0, 1, -1, 0, 1, 0, 0, 0, 0, 0, 0, 0, 0, 0, 0, 0),
+    (0, 1, -1, 0, 1, 0, 0, 0, 0, 0, 0, 0, 0, 0, 0, 0),
+)
+STEP2 = (
+    (0, 0, 0, 1, 0, 1, 1, 1, -1, -1, -1, -1, 1, 1, 1, 1),
+    (0, 0, 0, 1, 0, 1, 1, 1, -1, -1, -1, -1, 1, 1, 1, 1),
+    (0, 0, 0, 1, 0, 1, 1, 1, -1, -1, -1, -1, 1, 1, 1, 1),
+    (0, 0, 0, 1, 0, 1, 1, 1, -1, -1, -1, -1, 1, 1, 1, 1),
+)
 WAVES = 16
 AHEAD = 3
 PIECES = 4
 
 
-def look_up(table, w):
+def pack(values, width):
+    per = 30 // width
+    return [sum(v * 2 ** (width * k) for k, v in enumerate(values[i:i + per])) for i in range(0, len(values), per)]
+
+
+def unpack(words, w, width):
+    per = 30 // width
     if isinstance(w, int):
-        return table[w]
-    value = jnp.int32(table[0])
-    for k in range(1, len(table)):
-        if table[k] != table[0]:
-            value = jnp.where(w == k, jnp.int32(table[k]), value)
-    return value
+        word, w = words[w // per], w % per
+    else:
+        word, base = jnp.int32(words[0]), jnp.int32(0)
+        for k in range(1, len(words)):
+            word = jnp.where(w >= k * per, jnp.int32(words[k]), word)
+            base = jnp.where(w >= k * per, jnp.int32(k * per), base)
+        w = w - base
+    return (jnp.int32(word) >> (width * w)) & (2 ** width - 1)
 
 
 def kernel(a_ref, b_ref, out_ref, g, p, s, r, f, a_hi, a_lo, b_hi, b_lo,
-           in_sem, g_send, g_recv, s_send, s_recv, z_send, r_recv, f_recv, out_sem):
+           in_sem, g_send, g_recv, s_send, s_recv, z_send, r_recv, f_recv):
     row, core, z = lax.axis_index("row"), lax.axis_index("col"), lax.axis_index("depth")
     y, x = row // 4, row % 4
     piece_rows = a_ref.shape[1]
@@ -64,20 +97,39 @@
     def sign(q):
         return 1 - 2 * (q % 2)
 
-    def gather_copy(w, q):
-        s1, s2 = sign(q) * look_up(STEP1, w), sign(q) * look_up(STEP2, w)
+    plane = [(y * 4 + ((x + 1) & 3)), (y * 4 + ((x + 3) & 3)), (((y + 1) & 3) * 4 + x), (((y + 3) & 3) * 4 + x)]
+    words = pack(plane, 4)
+
+    def link(q, w):
+        s1, s2 = sign(q) * STEP1[q][w], sign(q) * STEP2[q][w]
         sx, sy = (s1, s2) if q < 2 else (s2, s1)
+        return 0 if sx == 1 else 1 if sx == -1 else 2 if sy == 1 else 3
+
+    links = [pack([link(q, w) for w in range(WAVES)], 2) for q in range(PIECES)]
+    parents = [pack(PARENT[q], 4) for q in range(PIECES)]
+
+    def gather_copy(w, q, own=False):
         return pltpu.make_async_remote_copy(
-            src_ref=g.at[look_up(PARENT, w), q], dst_ref=g.at[w, q], send_sem=g_send.at[w, q], recv_sem=g_recv.at[w, q],
-            device_id=at_row(y + sy, x + sx), device_id_type=MESH,
-        )
+            src_ref=a_ref.at[q] if own else g.at[unpack(parents[q], w, 4), q], dst_ref=g.at[w, q],
+            send_sem=g_send.at[w, q], recv_sem=g_recv.at[w, q],
+            device_id={"row": unpack(words, unpack(links[q], w, 2), 4)}, device_id_type=MESH,
+        )
+
+    codes, pairs = [], []
+    for q in range(PIECES):
+        values = []
+        for w in range(WAVES):
+            dx, dy = (D1[q][w], D2[q][w]) if q < 2 else (D2[q][w], D1[q][w])
+            xs, ys = (x + 4 - sign(q) * dx) & 3, (y + 4 - sign(q) * dy) & 3
+            keep = 1 - (((ys >> 1) + core) & 1)
+            kind = ((2 * (ys & 1) + (xs >> 1) - z + 4) * sign(q) + 16) & 3
+            values.append(keep + 2 * kind + 8 * (xs & 1))
+        codes.append(pack(values, 4))
+        pairs.append(pack([D1[q][w] * 2 + D2[q][w] % 2 if q < 2 else (D1[q][w] % 2) * 4 + D2[q][w] for w in range(WAVES)], 3))
 
     def origin(w, q):
-        d1, d2 = look_up(D1, w), look_up(D2, w)
-        dx, dy = (d1, d2) if q < 2 else (d2, d1)
-        xs, ys = (x + 8 - sign(q) * dx) % 4, (y + 8 - sign(q) * dy) % 4
-        pair = d1 * 2 + d2 % 2 if q < 2 else (d1 % 2) * 4 + d2
-        return ys // 2, 2 * (ys % 2) + xs // 2, xs % 2, pair
+        code = unpack(codes[q], w, 4)
+        return code & 7, code >> 3, unpack(pairs[q], w, 3)
 
     def core_copy(w, q, pair):
         return pltpu.make_async_remote_copy(
@@ -98,20 +150,13 @@
             recv_sem=f_recv.at[which, half, q], device_id={"depth": (z + 4 + step) % 4}, device_id_type=MESH,
         )
 
-    def out_copy(w, q, half):
-        return pltpu.make_async_copy(p.at[w, q], out_ref.at[half, q], out_sem.at[half, q])
-
-    def relation(dest_z, q):
-        return ((dest_z - z + 4) * sign(q) + 16) % 4
-
     def send_wave(w):
         for q in range(PIECES):
             gather_copy(w, q).start()
 
-    for copy in own:
-        copy.wait()
     for w in range(1, AHEAD + 1):
-        send_wave(w)
+        for q in range(PIECES):
+            gather_copy(w, q, own=True).start()
 
     for copy in b_copies:
         copy.wait()
@@ -122,6 +167,9 @@
         hi = b.astype(jnp.bfloat16)
         b_hi[pl.ds(pl.multiple_of(k * block_rows, 32), block_rows)] = hi
         b_lo[pl.ds(pl.multiple_of(k * block_rows, 32), block_rows)] = (b - hi.astype(jnp.float32)).astype(jnp.bfloat16)
+
+    for copy in own:
+        copy.wait()
 
     def multiply(w):
         for k0 in range(0, depth, 256):
@@ -137,27 +185,26 @@
 
     def stage_core(w):
         for q in range(PIECES):
-            dest_core, dest_z, half, pair = origin(w, q)
-            kind = relation(dest_z, q)
-
-            @pl.when(dest_core == core)
+            code, half, pair = origin(w, q)
+
+            @pl.when((code & 1) == 1)
             def _():
                 core_copy(w, q, pair).wait_recv()
                 p[w, q] = p[w, q] + s[pair, q]
 
-                @pl.when(kind == 2)
+                @pl.when(code == 5)
                 def _():
                     relay_copy(w, q, half).start()
 
-                @pl.when(kind == 3)
+                @pl.when(code == 7)
                 def _():
                     final_copy(w, q, half, 0).start()
 
     def stage_relay(w):
         for q in range(PIECES):
-            dest_core, dest_z, half, _ = origin(w, q)
-
-            @pl.when((dest_core == core) & (relation(dest_z, q) == 1))
+            code, half, _ = origin(w, q)
+
+            @pl.when(code == 3)
             def _():
                 relay_copy(w, q, half).wait_recv()
                 p[w, q] = p[w, q] + r[half, q]
@@ -165,14 +212,13 @@
 
     def stage_final(w):
         for q in range(PIECES):
-            dest_core, dest_z, half, _ = origin(w, q)
-
-            @pl.when((dest_core == core) & (relation(dest_z, q) == 0))
+            code, half, _ = origin(w, q)
+
+            @pl.when(code == 1)
             def _():
                 final_copy(w, q, half, 0).wait_recv()
                 final_copy(w, q, half, 1).wait_recv()
-                p[w, q] = p[w, q] + (f[0, half, q] + f[1, half, q])
-                out_copy(w, q, half).start()
+                out_ref[half, q] = p[w, q] + (f[0, half, q] + f[1, half, q])
 
     @pl.loop(0, WAVES + 3)
     def _(w):
@@ -201,9 +247,9 @@
 
             multiply(w)
             for q in range(PIECES):
-                dest_core, _, _, pair = origin(w, q)
-
-                @pl.when(dest_core != core)
+                code, _, pair = origin(w, q)
+
+                @pl.when((code & 1) == 0)
                 def _():
                     core_copy(w, q, pair).start()
 
@@ -222,7 +268,6 @@
             relay_copy(0, q, half).wait_send()
             final_copy(0, q, half, 0).wait_send()
             final_copy(0, q, half, 1).wait_send()
-            out_copy(0, q, half).wait()
 
 
 def per_device(amplitudes, intermediate):
@@ -233,9 +278,9 @@
     dma = pltpu.SemaphoreType.DMA
     result = pl.pallas_call(
         kernel,
-        out_shape=jax.ShapeDtypeStruct((2, PIECES, rows, columns), f32),
+        out_shape=pltpu.VMEM((2, PIECES, rows, columns), f32),
         in_specs=[pl.BlockSpec(memory_space=pl.ANY)] * 2,
-        out_specs=pl.BlockSpec(memory_space=pl.ANY),
+        out_specs=pl.BlockSpec(memory_space=pltpu.VMEM),
         scratch_shapes=[
             pltpu.VMEM((WAVES, PIECES, rows, depth), f32),
             pltpu.VMEM((WAVES, PIECES, rows, columns), f32),
@@ -254,7 +299,6 @@
             dma((3, 2, PIECES)),
             dma((2, PIECES)),
             dma((2, 2, PIECES)),
-            dma((2, PIECES)),
         ],
         compiler_params=pltpu.CompilerParams(
             collective_id=0, has_side_effects=True, vmem_limit_bytes=60 * 2**20

time: 157 us -> 155 us (0.987)
  no operation moved by 1% of the time
where the time goes in v2:
time: 155 us
  Pallas kernels  154 us (99%)
    pallas_call x1, Pallas kernels, per_device(): pl.pallas_call(kernel, out_shape=pltpu.VMEM((2, PIECES, rows, columns), f...  154 us

profile of v2, /device:TPU:1, one launch (start us, length us, event | category | flops | bytes accessed | tf_op | source)
XLA Modules:
  0.0 155.0 jit_solution(16638642540213731427)
XLA Ops:
  0.0 153.8 %shard_map.28 = f32[2,4,56,896]{3,2,1,0:T(8,128)S(1)} custom-call(f32[4,56,1792]{2,1,0:T(8,128)} %bitcast.3, f32[1792,896]{1,0:T(8,128)} %b_ref.1), custom_call_target="tpu_custom_call" | custom-call | flops 34500001792 | bytes 10000000 | tf_op jit(solution)/shard_map/pallas_call | solution.py:279
  153.9 1.2 copy.4

commit v3 on v2

--- a/solution.py
+++ b/solution.py
@@ -65,10 +65,75 @@
 def kernel(a_ref, b_ref, out_ref, g, p, s, r, f, a_hi, a_lo, b_hi, b_lo,
            in_sem, g_send, g_recv, s_send, s_recv, z_send, r_recv, f_recv):
     row, core, z = lax.axis_index("row"), lax.axis_index("col"), lax.axis_index("depth")
-    y, x = row // 4, row % 4
+    y, x = row >> 2, row & 3
     piece_rows = a_ref.shape[1]
     depth, columns = b_ref.shape
     block_rows = PIECES * piece_rows
+
+    def at_row(yy, xx):
+        return {"row": ((yy + 4) & 3) * 4 + ((xx + 4) & 3)}
+
+    barrier = pltpu.get_barrier_semaphore()
+    neighbours = [at_row(y, x + 1), at_row(y, x - 1), at_row(y + 1, x), at_row(y - 1, x),
+                  {"col": 1 - core}, {"depth": (z + 1) % 4}, {"depth": (z + 3) % 4}]
+    for device in neighbours:
+        pl.semaphore_signal(barrier, inc=1, device_id=device, device_id_type=MESH)
+    pl.semaphore_wait(barrier, len(neighbours))
+
+    def sign(q):
+        return 1 - 2 * (q % 2)
+
+    plane = [(y * 4 + ((x + 1) & 3)), (y * 4 + ((x + 3) & 3)), (((y + 1) & 3) * 4 + x), (((y + 3) & 3) * 4 + x)]
+    words = pack(plane, 4)
+
+    def link(q, w):
+        s1, s2 = sign(q) * STEP1[q][w], sign(q) * STEP2[q][w]
+        sx, sy = (s1, s2) if q < 2 else (s2, s1)
+        return 0 if sx == 1 else 1 if sx == -1 else 2 if sy == 1 else 3
+
+    links = [pack([link(q, w) for w in range(WAVES)], 2) for q in range(PIECES)]
+    parents = [pack(PARENT[q], 4) for q in range(PIECES)]
+
+    def gather_copy(w, q, own=False):
+        return pltpu.make_async_remote_copy(
+            src_ref=a_ref.at[q] if own else g.at[unpack(parents[q], w, 4), q], dst_ref=g.at[w, q],
+            send_sem=g_send.at[w, q], recv_sem=g_recv.at[w, q],
+            device_id={"row": unpack(words, unpack(links[q], w, 2), 4)}, device_id_type=MESH,
+        )
+
+    def origin(w, q):
+        code = unpack(codes[q], w, 4)
+        return code & 7, code >> 3, unpack(pairs[q], w, 3)
+
+    def core_copy(w, q, pair):
+        return pltpu.make_async_remote_copy(
+            src_ref=p.at[w, q], dst_ref=s.at[pair, q], send_sem=s_send.at[pair, q], recv_sem=s_recv.at[pair, q],
+            device_id={"col": 1 - core}, device_id_type=MESH,
+        )
+
+    cut = (columns // 256 + 1) // 2 * 256
+    parts = (pl.ds(0, cut), pl.ds(cut, columns - cut))
+
+    def relay_copy(w, q, half, i):
+        return pltpu.make_async_remote_copy(
+            src_ref=p.at[w, q, :, parts[i]], dst_ref=r.at[half, q, :, parts[i]], send_sem=z_send.at[i, 1, half, q],
+            recv_sem=r_recv.at[i, half, q], device_id={"depth": (z + 4 + sign(q)) & 3}, device_id_type=MESH,
+        )
+
+    def final_copy(w, q, half, which, i):
+        step = -sign(q) if which == 0 else sign(q)
+        return pltpu.make_async_remote_copy(
+            src_ref=p.at[w, q, :, parts[i]], dst_ref=f.at[which, half, q, :, parts[i]], send_sem=z_send.at[i, 2 * which, half, q],
+            recv_sem=f_recv.at[i, which, half, q], device_id={"depth": (z + 4 + step) & 3}, device_id_type=MESH,
+        )
+
+    def send_wave(w):
+        for q in range(PIECES):
+            gather_copy(w, q).start()
+
+    for w in range(1, AHEAD + 1):
+        for q in range(PIECES):
+            gather_copy(w, q, own=True).start()
 
     own = [pltpu.make_async_copy(a_ref.at[q], g.at[0, q], in_sem.at[q]) for q in range(PIECES)]
     for copy in own:
@@ -83,37 +148,6 @@
     ]
     for copy in b_copies:
         copy.start()
-
-    def at_row(yy, xx):
-        return {"row": ((yy + 8) % 4) * 4 + (xx + 8) % 4}
-
-    barrier = pltpu.get_barrier_semaphore()
-    neighbours = [at_row(y, x + 1), at_row(y, x - 1), at_row(y + 1, x), at_row(y - 1, x),
-                  {"col": 1 - core}, {"depth": (z + 1) % 4}, {"depth": (z + 3) % 4}]
-    for device in neighbours:
-        pl.semaphore_signal(barrier, inc=1, device_id=device, device_id_type=MESH)
-    pl.semaphore_wait(barrier, len(neighbours))
-
-    def sign(q):
-        return 1 - 2 * (q % 2)
-
-    plane = [(y * 4 + ((x + 1) & 3)), (y * 4 + ((x + 3) & 3)), (((y + 1) & 3) * 4 + x), (((y + 3) & 3) * 4 + x)]
-    words = pack(plane, 4)
-
-    def link(q, w):
-        s1, s2 = sign(q) * STEP1[q][w], sign(q) * STEP2[q][w]
-        sx, sy = (s1, s2) if q < 2 else (s2, s1)
-        return 0 if sx == 1 else 1 if sx == -1 else 2 if sy == 1 else 3
-
-    links = [pack([link(q, w) for w in range(WAVES)], 2) for q in range(PIECES)]
-    parents = [pack(PARENT[q], 4) for q in range(PIECES)]
-
-    def gather_copy(w, q, own=False):
-        return pltpu.make_async_remote_copy(
-            src_ref=a_ref.at[q] if own else g.at[unpack(parents[q], w, 4), q], dst_ref=g.at[w, q],
-            send_sem=g_send.at[w, q], recv_sem=g_recv.at[w, q],
-            device_id={"row": unpack(words, unpack(links[q], w, 2), 4)}, device_id_type=MESH,
-        )
 
     codes, pairs = [], []
     for q in range(PIECES):
@@ -127,37 +161,6 @@
         codes.append(pack(values, 4))
         pairs.append(pack([D1[q][w] * 2 + D2[q][w] % 2 if q < 2 else (D1[q][w] % 2) * 4 + D2[q][w] for w in range(WAVES)], 3))
 
-    def origin(w, q):
-        code = unpack(codes[q], w, 4)
-        return code & 7, code >> 3, unpack(pairs[q], w, 3)
-
-    def core_copy(w, q, pair):
-        return pltpu.make_async_remote_copy(
-            src_ref=p.at[w, q], dst_ref=s.at[pair, q], send_sem=s_send.at[pair, q], recv_sem=s_recv.at[pair, q],
-            device_id={"col": 1 - core}, device_id_type=MESH,
-        )
-
-    def relay_copy(w, q, half):
-        return pltpu.make_async_remote_copy(
-            src_ref=p.at[w, q], dst_ref=r.at[half, q], send_sem=z_send.at[1, half, q], recv_sem=r_recv.at[half, q],
-            device_id={"depth": (z + 4 + sign(q)) % 4}, device_id_type=MESH,
-        )
-
-    def final_copy(w, q, half, which):
-        step = -sign(q) if which == 0 else sign(q)
-        return pltpu.make_async_remote_copy(
-            src_ref=p.at[w, q], dst_ref=f.at[which, half, q], send_sem=z_send.at[2 * which, half, q],
-            recv_sem=f_recv.at[which, half, q], device_id={"depth": (z + 4 + step) % 4}, device_id_type=MESH,
-        )
-
-    def send_wave(w):
-        for q in range(PIECES):
-            gather_copy(w, q).start()
-
-    for w in range(1, AHEAD + 1):
-        for q in range(PIECES):
-            gather_copy(w, q, own=True).start()
-
     for copy in b_copies:
         copy.wait()
 
@@ -178,8 +181,8 @@
             a_hi[:, k0:k0 + 256] = hi
             a_lo[:, k0:k0 + 256] = (a - hi.astype(jnp.float32)).astype(jnp.bfloat16)
         dot = functools.partial(jnp.dot, preferred_element_type=jnp.float32)
-        for n0 in range(0, columns, 256):
-            n1 = min(n0 + 256, columns)
+        for n0 in range(0, columns, 512):
+            n1 = min(n0 + 512, columns)
             total = dot(a_hi[...], b_hi[:, n0:n1]) + (dot(a_hi[...], b_lo[:, n0:n1]) + dot(a_lo[...], b_hi[:, n0:n1]))
             p[w, :, :, n0:n1] = total.reshape(PIECES, piece_rows, n1 - n0)
 
@@ -194,21 +197,24 @@
 
                 @pl.when(code == 5)
                 def _():
-                    relay_copy(w, q, half).start()
+                    for i in range(2):
+                        relay_copy(w, q, half, i).start()
 
                 @pl.when(code == 7)
                 def _():
-                    final_copy(w, q, half, 0).start()
+                    for i in range(2):
+                        final_copy(w, q, half, 0, i).start()
 
     def stage_relay(w):
-        for q in range(PIECES):
-            code, half, _ = origin(w, q)
-
-            @pl.when(code == 3)
-            def _():
-                relay_copy(w, q, half).wait_recv()
-                p[w, q] = p[w, q] + r[half, q]
-                final_copy(w, q, half, 1).start()
+        for i in range(2):
+            for q in range(PIECES):
+                code, half, _ = origin(w, q)
+
+                @pl.when(code == 3)
+                def _():
+                    relay_copy(w, q, half, i).wait_recv()
+                    p[w, q, :, parts[i]] = p[w, q, :, parts[i]] + r[half, q, :, parts[i]]
+                    final_copy(w, q, half, 1, i).start()
 
     def stage_final(w):
         for q in range(PIECES):
@@ -216,8 +222,9 @@
 
             @pl.when(code == 1)
             def _():
-                final_copy(w, q, half, 0).wait_recv()
-                final_copy(w, q, half, 1).wait_recv()
+                for i in range(2):
+                    for which in range(2):
+                        final_copy(w, q, half, which, i).wait_recv()
                 out_ref[half, q] = p[w, q] + (f[0, half, q] + f[1, half, q])
 
     @pl.loop(0, WAVES + 3)
@@ -265,9 +272,10 @@
 
     for half in range(2):
         for q in range(PIECES):
-            relay_copy(0, q, half).wait_send()
-            final_copy(0, q, half, 0).wait_send()
-            final_copy(0, q, half, 1).wait_send()
+            for i in range(2):
+                relay_copy(0, q, half, i).wait_send()
+                final_copy(0, q, half, 0, i).wait_send()
+                final_copy(0, q, half, 1, i).wait_send()
 
 
 def per_device(amplitudes, intermediate):
@@ -296,9 +304,9 @@
             dma((WAVES, PIECES)),
             dma((WAVES // 2, PIECES)),
             dma((WAVES // 2, PIECES)),
-            dma((3, 2, PIECES)),
-            dma((2, PIECES)),
+            dma((2, 3, 2, PIECES)),
             dma((2, 2, PIECES)),
+            dma((2, 2, 2, PIECES)),
         ],
         compiler_params=pltpu.CompilerParams(
             collective_id=0, has_side_effects=True, vmem_limit_bytes=60 * 2**20

time: 155 us -> 155 us (level)
  no operation moved by 1% of the time
where the time goes in v3:
time: 155 us; the launch traced here: 154 us
  Pallas kernels  153 us (99%)
    pallas_call x1, Pallas kernels, per_device(): pl.pallas_call(kernel, out_shape=pltpu.VMEM((2, PIECES, rows, columns), f...  153 us

profile of v3, /device:TPU:1, one launch (start us, length us, event | category | flops | bytes accessed | tf_op | source)
XLA Modules:
  0.0 154.5 jit_solution(11656991745949778598)
XLA Ops:
  0.0 153.3 %shard_map.28 = f32[2,4,56,896]{3,2,1,0:T(8,128)S(1)} custom-call(f32[4,56,1792]{2,1,0:T(8,128)} %bitcast.3, f32[1792,896]{1,0:T(8,128)} %b_ref.1), custom_call_target="tpu_custom_call" | custom-call | flops 34500001792 | bytes 10000000 | tf_op jit(solution)/shard_map/pallas_call | solution.py:287
  153.3 1.2 copy.4

commit v4 on v3

--- a/solution.py
+++ b/solution.py
@@ -181,28 +181,28 @@
             a_hi[:, k0:k0 + 256] = hi
             a_lo[:, k0:k0 + 256] = (a - hi.astype(jnp.float32)).astype(jnp.bfloat16)
         dot = functools.partial(jnp.dot, preferred_element_type=jnp.float32)
-        for n0 in range(0, columns, 512):
-            n1 = min(n0 + 512, columns)
+        for n0 in range(0, columns, 256):
+            n1 = min(n0 + 256, columns)
             total = dot(a_hi[...], b_hi[:, n0:n1]) + (dot(a_hi[...], b_lo[:, n0:n1]) + dot(a_lo[...], b_hi[:, n0:n1]))
             p[w, :, :, n0:n1] = total.reshape(PIECES, piece_rows, n1 - n0)
 
     def stage_core(w):
-        for q in range(PIECES):
-            code, half, pair = origin(w, q)
-
-            @pl.when((code & 1) == 1)
-            def _():
-                core_copy(w, q, pair).wait_recv()
-                p[w, q] = p[w, q] + s[pair, q]
-
-                @pl.when(code == 5)
+        for i in range(2):
+            for q in range(PIECES):
+                code, half, pair = origin(w, q)
+
+                @pl.when((code & 1) == 1)
                 def _():
-                    for i in range(2):
+                    if i == 0:
+                        core_copy(w, q, pair).wait_recv()
+                        p[w, q] = p[w, q] + s[pair, q]
+
+                    @pl.when(code == 5)
+                    def _():
                         relay_copy(w, q, half, i).start()
 
-                @pl.when(code == 7)
-                def _():
-                    for i in range(2):
+                    @pl.when(code == 7)
+                    def _():
                         final_copy(w, q, half, 0, i).start()
 
     def stage_relay(w):

time: 155 us -> 157 us (1.013)
  Pallas kernels: 153 us -> 155 us
    pallas_call x1, Pallas kernels: 153 us -> 155 us  [per_device(): pl.pallas_call(kernel, out_shape=pltpu.VMEM((2, PIECES, rows, columns), f...]
where the time goes in v4:
time: 157 us
  Pallas kernels  155 us (99%)
    pallas_call x1, Pallas kernels, per_device(): pl.pallas_call(kernel, out_shape=pltpu.VMEM((2, PIECES, rows, columns), f...  155 us

profile of v4, /device:TPU:1, one launch (start us, length us, event | category | flops | bytes accessed | tf_op | source)
XLA Modules:
  0.0 156.5 jit_solution(5056714318452139831)
XLA Ops:
  0.0 155.4 %shard_map.28 = f32[2,4,56,896]{3,2,1,0:T(8,128)S(1)} custom-call(f32[4,56,1792]{2,1,0:T(8,128)} %bitcast.3, f32[1792,896]{1,0:T(8,128)} %b_ref.1), custom_call_target="tpu_custom_call" | custom-call | flops 34500001792 | bytes 10000000 | tf_op jit(solution)/shard_map/pallas_call | solution.py:287
  155.4 1.2 copy.4
